TPU v7x, 32 devices: a whole 2x2x4 slice. The times are simulated.
32 devices in a mesh: wide: 16 (over z, y, core), narrow: 2 (over x).
Axes of the slice: x: 2, y: 2, z: 4, core: 2. Of those that a mesh axis runs over, the one named last changes fastest.
Arguments:
- tokens: bfloat16 [32, 512, 768], P(('wide', 'narrow')), may hold values from -6 to 6
- lengths: int32 [32], P(('wide', 'narrow')), may hold values from 128 to 512, as said below
- w_qkv: bfloat16 [768, 2304], P('wide'), may hold values from -0.21875 to 0.21875
- w_out: bfloat16 [768, 768], P('wide'), may hold values from -1.75 to 1.75
- w_in: bfloat16 [768, 3072], P('wide'), may hold values from -0.21875 to 0.21875
- w_down: bfloat16 [3072, 768], P('wide'), may hold values from -0.109375 to 0.109375
- norms_biases: bfloat16 [9216], P('wide'), may hold values from -0.4 to 1.6, as said below
- cotangent: bfloat16 [32, 512, 768], P(('wide', 'narrow')), may hold values from -6 to 6
Outputs:
- output: bfloat16 [32, 512, 768], P(('wide', 'narrow'))
- grad_tokens: float32 [32, 512, 768], P(('wide', 'narrow'))
- grad_qkv: float32 [768, 2304], P('wide')
- grad_out: float32 [768, 768], P('wide')
- grad_in: float32 [768, 3072], P('wide')
- grad_down: float32 [3072, 768], P('wide')
- grad_norms_biases: float32 [9216], P('wide')
Inputs may be any that keep to these rules, and one draw needn't show every extreme that they name: `lengths`: the number of real tokens of each sequence; keys at positions at or past it are padding; some sequence has 512 and some has 128. `norms_biases`: the gains g1 and g2 lie within 0.6 and 1.6, the biases and shifts within -0.4 and 0.4.
All inputs are finite; a program needn't handle non-finite values.
Results may differ from a plain program's by a relative error of at most 0.019.
Values may be sent and summed in bfloat16 or wider, within the bound.
A program may use at most 128 MiB of HBM per device.

v0:
```python
import functools

import jax
import jax.numpy as jnp
import numpy as np
from jax import lax
from jax.experimental import pallas as pl
from jax.experimental.pallas import tpu as pltpu
from jax.sharding import PartitionSpec as P

HEADS = 12
MESH = pl.DeviceIdType.MESH
BF = jnp.bfloat16
F32 = jnp.float32
NT = (((1,), (1,)), ((), ()))
TN = (((0,), (0,)), ((), ()))
ZH, ZL, YS, CS = 2, 2, 2, 2
ZS = ZH * ZL
QKV, OUT, IN, DOWN, CHUNKS = 0, 3, 4, 8, 12
RING = 8
(
    S_E1, S_EO, S_E2, S_E3, S_E4, S_E5, S_R0, S_R1, S_R2A, S_R2B, S_R3A,
    S_R3B, S_R4A, S_R4B, S_R5, S_SPREAD, S_PROJECT, S_ATTEND, S_OUT, S_UP, S_DOWN, S_NORM2,
    S_GDOWN, S_GACT, S_GIN, S_GNORM, S_NORM1, S_GOUT, S_GCTX, S_ABACK, S_GQKV, S_GGRADS, S_GX,
) = range(33)
GATHERED = (
    (0, 0, 384), (0, 384, 384), (1, 0, 384), (1, 384, 384), (2, 0, 384), (2, 384, 384), (3, 0, 384), (3, 384, 384),
    (4, 0, 384), (4, 384, 384), (5, 0, 384), (5, 384, 384), (6, 0, 384), (6, 384, 384), (7, 0, 384), (7, 384, 384),
    (8, 0, 384), (8, 384, 384), (9, 0, 384), (9, 384, 384), (10, 0, 384), (10, 384, 384), (11, 0, 384), (11, 384, 384),
)
SUMMED = (
    (0, 0, 384), (1, 0, 384), (2, 0, 384), (3, 0, 384), (4, 0, 384), (5, 0, 384), (6, 0, 384), (7, 0, 384),
    (8, 0, 384), (9, 0, 384), (10, 0, 384), (11, 0, 384),
)
ORDER = (
    (S_EO, 0), (S_E1, 0), (S_EO, 1), (S_E1, 1), (S_E1, 2), (S_EO, 2), (S_EO, 3), (S_E1, 3), (S_EO, 4), (S_EO, 5),
    (S_E2, 0), (S_E1, 4), (S_EO, 6), (S_E2, 1), (S_E1, 5), (S_EO, 7), (S_E3, 0), (S_E2, 2), (S_E1, 6), (S_EO, 8),
    (S_E3, 1), (S_E2, 3), (S_E4, 0), (S_E1, 7), (S_EO, 9), (S_E5, 0), (S_E3, 2), (S_E2, 4), (S_E4, 1), (S_E1, 8),
    (S_EO, 10), (S_E5, 1), (S_E3, 3), (S_SPREAD, 0), (S_E4, 2), (S_E2, 5), (S_E1, 9), (S_EO, 11), (S_PROJECT, 0), (S_E5, 2),
    (S_E3, 4), (S_E4, 3), (S_E2, 6), (S_E1, 10), (S_EO, 12), (S_ATTEND, 0), (S_E5, 3), (S_E4, 4), (S_E3, 5), (S_E3, 6),
    (S_E2, 7), (S_E2, 8), (S_E1, 11), (S_E1, 12), (S_E5, 4), (S_EO, 13), (S_EO, 14), (S_PROJECT, 1), (S_E2, 9), (S_E4, 5),
    (S_E1, 13), (S_EO, 15), (S_ATTEND, 1), (S_E5, 5), (S_E4, 6), (S_E3, 7), (S_E3, 8), (S_E2, 10), (S_E1, 14), (S_E2, 11),
    (S_E1, 15), (S_E5, 6), (S_EO, 16), (S_EO, 17), (S_PROJECT, 2), (S_E3, 9), (S_E4, 7), (S_E2, 12), (S_E1, 16), (S_EO, 18),
    (S_ATTEND, 2), (S_E5, 7), (S_E4, 8), (S_E4, 9), (S_E3, 10), (S_E3, 11), (S_E2, 13), (S_E2, 14), (S_E1, 17), (S_E5, 8),
    (S_E1, 18), (S_E5, 9), (S_E3, 12), (S_EO, 19), (S_EO, 20), (S_OUT, 0), (S_E4, 10), (S_E3, 13), (S_E4, 11), (S_E2, 15),
    (S_E2, 16), (S_E5, 10), (S_E1, 19), (S_E1, 20), (S_E5, 11), (S_E3, 14), (S_EO, 21), (S_EO, 22), (S_UP, 0), (S_E4, 12),
    (S_E2, 17), (S_E4, 13), (S_E3, 15), (S_E1, 21), (S_E5, 12), (S_E2, 18), (S_E5, 13), (S_E1, 22), (S_EO, 23), (S_UP, 1),
    (S_E4, 14), (S_E3, 16), (S_E2, 19), (S_E1, 23), (S_UP, 2), (S_E5, 14), (S_E4, 15), (S_E3, 17), (S_E2, 20), (S_E3, 18),
    (S_E4, 16), (S_E5, 15), (S_UP, 3), (S_E5, 16), (S_E4, 17), (S_E3, 19), (S_E2, 21), (S_E2, 22), (S_E5, 17), (S_E3, 20),
    (S_E4, 18), (S_DOWN, 0), (S_E4, 19), (S_E5, 18), (S_E2, 23), (S_E3, 21), (S_E5, 19), (S_DOWN, 1), (S_E3, 22), (S_E4, 20),
    (S_E3, 23), (S_E5, 20), (S_E4, 21), (S_E4, 22), (S_E5, 21), (S_DOWN, 2), (S_E5, 22), (S_E4, 23), (S_E5, 23), (S_DOWN, 3),
    (S_NORM2, 0), (S_GDOWN, 0), (S_R0, 0), (S_GDOWN, 1), (S_GACT, 0), (S_R1, 0), (S_R0, 1), (S_GDOWN, 2), (S_GDOWN, 3), (S_R0, 2),
    (S_R0, 3), (S_R1, 1), (S_GACT, 1), (S_GACT, 2), (S_GACT, 3), (S_R2A, 0), (S_R1, 3), (S_GNORM, 0), (S_R1, 2), (S_GIN, 0),
    (S_R2A, 1), (S_GIN, 1), (S_R2B, 1), (S_R2B, 0), (S_R0, 4), (S_GNORM, 1), (S_R2A, 3), (S_GIN, 2), (S_GIN, 3), (S_R2B, 3),
    (S_R0, 5), (S_R2A, 2), (S_GNORM, 2), (S_GNORM, 3), (S_R0, 6), (S_R0, 7), (S_R1, 4), (S_R3B, 1), (S_NORM1, 0), (S_GOUT, 0),
    (S_R1, 6), (S_R3B, 0), (S_R0, 8), (S_R3B, 3), (S_R1, 5), (S_GCTX, 0), (S_R3A, 3), (S_R1, 8), (S_R2A, 4), (S_ABACK, 0),
    (S_R2A, 6), (S_ABACK, 1), (S_R2A, 5), (S_R1, 7), (S_R2B, 2), (S_GQKV, 0), (S_R2B, 5), (S_R3A, 2), (S_R4B, 3), (S_R2A, 8),
    (S_ABACK, 2), (S_R2A, 7), (S_R0, 9), (S_R2B, 4), (S_GQKV, 1), (S_R3B, 2), (S_R2B, 7), (S_R2B, 8), (S_GQKV, 2), (S_R1, 9),
    (S_R2B, 6), (S_R3B, 5), (S_R3A, 5), (S_GX, 0), (S_R0, 10), (S_R3A, 1), (S_R4A, 3), (S_R3B, 4), (S_GGRADS, 0), (S_R4B, 0),
    (S_R3A, 8), (S_R3B, 8), (S_R0, 11), (S_R3B, 7), (S_GX, 1), (S_R2B, 9), (S_R1, 11), (S_R2A, 9), (S_R3B, 6), (S_R5, 0),
    (S_R1, 10), (S_R3A, 6), (S_GX, 2), (S_R3A, 7), (S_R3B, 9), (S_R4B, 7), (S_R2A, 11), (S_R2B, 11), (S_R5, 3), (S_R3A, 4),
    (S_R4B, 8), (S_R4A, 2), (S_R4A, 1), (S_R4B, 1), (S_R3A, 0), (S_R4B, 5), (S_R2B, 10), (S_R2A, 10), (S_R4B, 4), (S_R3A, 9),
    (S_R4B, 2), (S_R3B, 11), (S_R4A, 5), (S_R4B, 9), (S_R5, 1), (S_R4A, 0), (S_R4A, 7), (S_R3B, 10), (S_R4A, 4), (S_R3A, 11),
    (S_R5, 9), (S_R3A, 10), (S_R4A, 8), (S_R4A, 9), (S_R4B, 6), (S_R5, 4), (S_R4A, 11), (S_R5, 7), (S_R4B, 11), (S_R5, 2),
    (S_R5, 6), (S_R5, 8), (S_R4B, 10), (S_R4A, 10), (S_R5, 5), (S_R4A, 6), (S_R5, 11), (S_R5, 10),
)
SQRT_HALF = 0.7071067811865476
INV_SQRT_TAU = 0.3989422804014327


def dot(left, right, dims=None):
    if dims is None:
        return jnp.dot(left, right, preferred_element_type=F32)
    return lax.dot_general(left, right, dims, preferred_element_type=F32)


def loop(count, body):
    def step(index, carry):
        body(index)
        return carry

    lax.fori_loop(0, count, step, 0)


def span(index, size):
    return pl.ds(pl.multiple_of(index * size, size), size)


def layer_kernel(
    x_hbm, len_ref, wqkv_hbm, wout_hbm, win_hbm, wdown_hbm, vec_hbm, cot_hbm,
    out_hbm, gtok_hbm, gqkv_hbm, gout_hbm, gin_hbm, gdown_hbm, gvec_hbm,
    wa, wd, vb, gd, go, gv, rcore, rya, rxb, rza, ryb, rzb, rxa, rfb, rv_core, rv_y, rv_z, rv_x, fin, vec,
    x, cot, qkv, vt, pt, ct, n1, y1b, y1t, act, dact, h2, dfb, dcx, rs1, prm, vg,
    s_load, s_io, s_store,
    g_sent, grz, gry, grx, grc, v_sent, vrz, vry, vrc,
    r_sent, rv_sent, rrc, rry, rrx, rrz, rrf, wrc, wry, wrz, wrx,
):
    seq, model = x.shape
    rows = wa.shape[-2]
    hidden = dact.shape[1]
    pair = 2 * (model // HEADS)
    head = model // HEADS
    group = model // 3
    half = model // 2
    wide = lax.axis_index("wide")
    px = lax.axis_index("narrow")
    c = lax.rem(wide, CS)
    y = lax.rem(wide // CS, YS)
    z = wide // (CS * YS)
    zl = lax.rem(z, ZL)
    zh = z // ZL

    def device(zz, yy, cc, xx):
        return ((zz * YS + yy) * CS + cc, xx)

    sibling = device(z, y, 1 - c, px)
    across_y = device(z, 1 - y, c, px)
    across_x = device(z, y, c, 1 - px)

    def ahead(dz):
        return lax.rem(z + dz, ZS)

    def behind(dz):
        return lax.rem(z + ZS - dz, ZS)

    def remote(src, dst, send, recv, where):
        return pltpu.make_async_remote_copy(
            src_ref=src, dst_ref=dst, send_sem=send, recv_sem=recv, device_id=where, device_id_type=MESH
        )

    ALL = slice(None)

    def drained(ref, sem):
        pltpu.make_async_copy(ref, ref, sem).wait()

    def rows_of(count, cols):
        return x.at[pl.ds(0, count), pl.ds(0, cols)]

    def load(src, dst, sem):
        cp = pltpu.make_async_copy(src, dst, sem)
        cp.start()
        return cp

    load_vec = load(vec_hbm, vec, s_io.at[2])
    load_x = load(x_hbm.at[0], x, s_io.at[0])
    for k in range(CHUNKS):
        if k < OUT:
            for part in range(3):
                load(
                    wqkv_hbm.at[:, pl.ds(part * model + k * group, group)],
                    wa.at[k, zh, zl, y, c, :, pl.ds(part * group, group)],
                    s_load.at[k],
                )
        elif k < IN:
            load(wout_hbm, wa.at[k, zh, zl, y, c], s_load.at[k])
        elif k < DOWN:
            load(win_hbm.at[:, pl.ds((k - IN) * model, model)], wa.at[k, zh, zl, y, c], s_load.at[k])
        else:
            load(wdown_hbm.at[pl.ds((k - DOWN) * rows, rows)], wd.at[zh, zl, y, c, k - DOWN], s_load.at[k])
    load_cot = load(cot_hbm.at[0], cot, s_io.at[1])

    barrier = pltpu.get_barrier_semaphore()
    for where in (sibling, across_y, across_x, *(device(ahead(dz), y, c, px) for dz in (1, 2, 3))):
        pl.semaphore_signal(barrier, inc=1, device_id=where, device_id_type=MESH)
    pl.semaphore_wait(barrier, 6)

    third = rows // 3
    kept = pl.ds(pl.multiple_of(px * third, third), 2 * third)
    given = pl.ds(pl.multiple_of(px * 2 * third, third), third)
    taken = pl.ds(pl.multiple_of((1 - px) * 2 * third, third), third)

    def wcut(i, zz, yy, cc, r=ALL):
        k, first, count = GATHERED[i]
        cols = pl.ds(first, count)
        zi = (ALL, ALL) if zz is None else (zz // ZL, lax.rem(zz, ZL))
        if k < DOWN:
            return wa.at[(k, *zi, yy, cc, r, cols)]
        return wd.at[(*zi, yy, cc, k - DOWN, r, cols)]

    def g_z(i, dz, source):
        piece = wcut(i, source, y, c, kept)
        return remote(piece, piece, g_sent.at[i], grz.at[i], device(ahead(dz), y, c, px))

    def g_y(i, dz, column):
        piece = wcut(i, behind(dz), column, c, kept)
        return remote(piece, piece, g_sent.at[i], gry.at[i], across_y)

    def g_x1(i, dz, r):
        piece = wcut(i, behind(dz), y, c, r)
        return remote(piece, piece, g_sent.at[i], grx.at[i], across_x)

    def g_x2(i, r):
        piece = wcut(i, None, 1 - y, c, r)
        return remote(piece, piece, g_sent.at[i], grx.at[i], across_x)

    def g_core(i, core):
        piece = wcut(i, None, ALL, core)
        return remote(piece, piece, g_sent.at[i], grc.at[i], sibling)

    def v_z(dz, source):
        piece = vb.at[source // ZL, lax.rem(source, ZL), y, c]
        return remote(piece, piece, v_sent, vrz, device(ahead(dz), y, c, px))

    def v_y(column):
        piece = vb.at[:, :, column, c]
        return remote(piece, piece, v_sent, vry, across_y)

    def v_core(core):
        piece = vb.at[:, :, :, core]
        return remote(piece, piece, v_sent, vrc, sibling)

    loaded = set()

    def own(k):
        if k not in loaded:
            loaded.add(k)
            drained(rows_of(rows, model), s_load.at[k])

    def e1(i):
        own(GATHERED[i][0])
        for dz in (1, 2, 3):
            g_z(i, dz, z).start()
        if i == 1:
            load_vec.wait()
            segment = vec.shape[0] // 3
            row = vec[...].astype(F32).reshape(1, -1)
            vb[zh, zl, y, c] = jnp.zeros(vb.shape[-2:], BF)
            for s in range(3):
                vb[zh, zl, y, c, s : s + 1, 0:segment] = row[:, s * segment : (s + 1) * segment].astype(BF)
            for dz in (1, 2, 3):
                v_z(dz, z).start()

    def eo(i):
        own(GATHERED[i][0])
        g_y(i, 0, y).start()

    def e2(i):
        if i == 1:
            drained(rv_z, vrz)
            v_y(y).start()
        drained(rows_of(3 * 2 * third, GATHERED[i][2]), grz.at[i])
        for dz in (1, 2, 3):
            g_y(i, dz, y).start()
            g_x1(i, dz, given).start()

    def e3(i):
        if i == 1:
            v_y(1 - y).wait_recv()
            v_core(c).start()
        drained(rows_of(ZS * 2 * third, GATHERED[i][2]), gry.at[i])
        g_x2(i, given).start()

    def e4(i):
        drained(rows_of((ZS + ZS - 1) * third, GATHERED[i][2]), grx.at[i])
        g_core(i, c).start()

    def e5(i):
        if i == 1:
            v_core(1 - c).wait_recv()
        g_core(i, 1 - c).wait_recv()

    def sent(*chunks):
        count = (3 + ZS) * 2 * third + (2 * ZS - 1) * third + ZS * YS * rows
        for i, (k, _, cols) in enumerate(GATHERED):
            if k in chunks:
                drained(qkv.at[:, pl.ds(0, count // 3), pl.ds(0, cols)], g_sent.at[i])

    def vec_sent():
        drained(x.at[pl.ds(0, 80)], v_sent)

    def place_matrix(k, lanes):
        i = lax.broadcasted_iota(jnp.int32, (lanes, model), 0)
        j = lax.broadcasted_iota(jnp.int32, (lanes, model), 1)
        quarter = model // 4
        return jnp.where((i < quarter) & (j == i + k * quarter), 1.0, 0.0).astype(BF)

    def pick_matrix(k, count, total, slot):
        b = lax.broadcasted_iota(jnp.int32, (count, total), 0)
        r = lax.broadcasted_iota(jnp.int32, (count, total), 1)
        segment = 4 * b + k
        return jnp.where((r == slot * (segment // 3) + lax.rem(segment, 3)) & (b < 12), 1.0, 0.0).astype(BF)

    def spread_params(_):
        lanes = vb.shape[-1]
        segments = vb[...].reshape(-1, lanes)
        total = None
        for k in range(4):
            picked = dot(pick_matrix(k, 16, segments.shape[0], vb.shape[-2]), segments).astype(BF)
            part = dot(picked, place_matrix(k, lanes))
            total = part if total is None else total + part
        prm[...] = total

    def gather_grads(_):
        lanes = gv.shape[-1]
        low = vg[...].astype(BF)
        total = None
        for k in range(4):
            cut = dot(low, place_matrix(k, lanes), NT).astype(BF)
            part = dot(pick_matrix(k, 16, 16 * gv.shape[-2], gv.shape[-2]), cut, TN)
            total = part if total is None else total + part
        gv[...] = total.astype(BF).reshape(gv.shape)

    def weight(k, cols=ALL):
        block = wa[k, :, :, :, :, :, cols]
        return block.reshape(-1, block.shape[-1])

    def project(g):
        grouped = span(g, group)

        def tile(part):
            cols = span(part, group)
            bias = jnp.where(part == 0, prm[0:1, grouped], jnp.where(part == 2, prm[1:2, grouped], 0.0))
            low = (dot(x[...], weight(g, cols)) + bias).astype(BF)
            qkv[g, :, cols] = low * jnp.where(part == 0, head**-0.5, 1.0).astype(BF)

        loop(3, tile)
        vt[grouped, :] = qkv[g, :, 2 * group :].T

    def attend(g):
        length = len_ref[0]

        def one(h):
            cols = span(h // 2, pair)
            keys = pl.ds(pl.multiple_of(group + (h // 2) * pair, pair), pair)
            lane = lax.broadcasted_iota(jnp.int32, (seq, pair), 1) // head
            masked = jnp.where(lane == lax.rem(h, 2), qkv[g, :, keys], jnp.zeros((), BF))
            scores = dot(masked, qkv[g, :, cols], NT)
            key = lax.broadcasted_iota(jnp.int32, scores.shape, 0)
            scores = jnp.where(key < length, scores, -1000000000.0)
            raised = jnp.exp(scores - jnp.max(scores, axis=0, keepdims=True))
            probs = (raised * (1.0 / jnp.sum(raised, axis=0, keepdims=True))).astype(BF)
            pt[g, h] = probs
            mine = pl.ds(pl.multiple_of(g * group + h * head, head), head)
            ct[mine, :] = dot(vt[mine, :], probs).astype(BF)

        loop(group // head, one)

    def out_proj(_):
        context = ct[...].T
        bo, g1, c1 = prm[2:3, :], prm[3:4, :], prm[4:5, :]
        w = weight(OUT)

        def tile(i):
            r = span(i, 128)
            h1 = x[r, :].astype(F32) + (h2[r, :] + bo)
            centred = h1 - jnp.mean(h1, -1, keepdims=True)
            inverse = lax.rsqrt(jnp.mean(centred * centred, -1, keepdims=True) + 1e-06)
            normed = centred * inverse
            n1[r, :] = normed
            rs1[r, :] = inverse
            y1b[r, :] = (normed * g1 + c1).astype(BF)

        h2[...] = dot(context, w)
        loop(seq // 128, tile)

    def feed_up(j):
        def tile(t):
            cols = span(t, half)
            wide_cols = pl.ds(pl.multiple_of(j * model + t * half, half), half)
            u = dot(y1b[...], weight(IN + j, cols)) + prm[8 + j : 9 + j, cols]
            phi = 0.5 * (1.0 + lax.erf(u * SQRT_HALF))
            act[2 * j + t] = (u * phi).astype(BF).T.reshape(CS, 4, rows, seq)
            dact[:, wide_cols] = (phi + u * (jnp.exp(-0.5 * u * u) * INV_SQRT_TAU)).astype(BF)

        loop(2, tile)

    def act_rows(m):
        return act[:, :, m].reshape(-1, seq)

    def feed_down(m):
        w = wd[:, :, :, :, m].reshape(-1, model)
        part = dot(act_rows(m), w, TN)
        if m == 0:
            h2[...] = part + (n1[...] * prm[3:4, :] + prm[4:5, :]) + prm[5:6, :]
        else:
            h2[...] += part

    def vsum(row, value):
        vg[row : row + 1, :] += jnp.sum(value, axis=0, keepdims=True)

    def norm_back(dn, n, inverse):
        return (dn - jnp.mean(dn, -1, keepdims=True) - n * jnp.mean(dn * n, -1, keepdims=True)) * inverse

    def norm_two(_):
        g2, c2 = prm[6:7, :], prm[7:8, :]

        def tile(i):
            r = span(i, 128)
            h = h2[r, :]
            centred = h - jnp.mean(h, -1, keepdims=True)
            inverse = lax.rsqrt(jnp.mean(centred * centred, -1, keepdims=True) + 1e-06)
            n = centred * inverse
            dcx[r, :] = (n * g2 + c2).astype(BF)
            dy = cot[r, :].astype(F32)
            vsum(6, dy * n)
            vsum(7, dy)
            dh = norm_back(dy * g2, n, inverse)
            h2[r, :] = dh
            low = dh.astype(BF)
            dfb[r, :] = low
            vsum(5, low.astype(F32))

        loop(seq // 128, tile)
        store_out.append(store(dcx, out_hbm.at[0], 1))

    def grad_down(m):
        gd[m] = dot(act_rows(m), dfb[...]).astype(BF).reshape(gd.shape[1:])

    def grad_act(j):
        def tile(t):
            i = 2 * j + t
            cols = span(i, 2 * 4 * rows)
            zz = i // YS
            w = wd[zz // ZL, lax.rem(zz, ZL), lax.rem(i, YS)].reshape(2 * 4 * rows, model)
            du = (dot(dfb[...], w, NT) * dact[:, cols].astype(F32)).astype(BF)
            dact[:, cols] = du
            total = jnp.sum(du.astype(F32), axis=0, keepdims=True)
            vg[8 + j : 9 + j, t * half : (t + 1) * half] = total

        tile(0)
        tile(1)

    def grad_in(j):
        if j == 0:
            sent(*range(DOWN, CHUNKS))
            y1t[...] = y1b[...].T

        def tile(t):
            wide_cols = pl.ds(pl.multiple_of(j * model + t * 256, 256), 256)
            g = dot(y1t[...], dact[:, wide_cols]).astype(BF)
            wd[:, :, :, :, j, :, span(t, 256)] = g.reshape(ZH, ZL, YS, CS, rows, 256)

        loop(model // 256, tile)

    def grad_normed(j):
        h2[...] += dot(dact[:, j * model : (j + 1) * model], weight(IN + j), NT)

    def norm_one_back(_):
        g1 = prm[3:4, :]

        def tile(i):
            r = span(i, 128)
            dy, n = h2[r, :], n1[r, :]
            vsum(3, dy * n)
            vsum(4, dy)
            dh = norm_back(dy * g1, n, rs1[r, :])
            h2[r, :] = dh
            low = dh.astype(BF)
            dfb[r, :] = low
            vsum(2, low.astype(F32))

        loop(seq // 128, tile)

    def grad_out(_):
        g = dot(ct[...], dfb[...]).astype(BF)
        go[0] = g.reshape(ZH, ZL, YS, CS, rows, model)

    def grad_context(_):
        store_out.pop().wait()
        vt[...] = x[...].T
        dcx[...] = dot(dfb[...], weight(OUT), NT).astype(BF)

    def attend_back(g):
        def one(j):
            cols = span(j, pair)
            keys = pl.ds(pl.multiple_of(group + j * pair, pair), pair)
            vals = pl.ds(pl.multiple_of(2 * group + j * pair, pair), pair)
            place = pl.ds(pl.multiple_of(g * group + j * pair, pair), pair)
            lane = lax.broadcasted_iota(jnp.int32, (seq, pair), 1) // head
            dc = dcx[:, place]
            q, k, v = qkv[g, :, cols], qkv[g, :, keys], qkv[g, :, vals]
            kt = k.T
            dk, dv, dq = [], [], []
            for e in range(2):
                probs = pt[g, 2 * j + e]
                dv.append(dot(probs, dc))
                dp = dot(jnp.where(lane == e, v, jnp.zeros((), BF)), dc, NT)
                p32 = probs.astype(F32)
                t = p32 * dp
                ds = (t - p32 * jnp.sum(t, axis=0, keepdims=True)).astype(BF)
                dk.append(dot(ds, q))
                dq.append((dot(kt[e * head : (e + 1) * head, :], ds) * head**-0.5).astype(BF))
            dv = jnp.where(lane == 0, dv[0], dv[1]).astype(BF)
            dq = jnp.concatenate(dq, axis=0).T
            qkv[g, :, cols] = dq
            qkv[g, :, keys] = jnp.where(lane == 0, dk[0], dk[1]).astype(BF)
            qkv[g, :, vals] = dv
            vg[0:1, place] = jnp.sum(dq.astype(F32), axis=0, keepdims=True)
            vg[1:2, place] = jnp.sum(dv.astype(F32), axis=0, keepdims=True)

        loop(group // pair, one)

    def grad_qkv(g):
        if g == 0:
            sent(*range(IN, DOWN))

        def tile(t):
            cols = span(t, group)
            r = dot(vt[...], qkv[g, :, cols]).astype(BF)
            wa[IN + g, :, :, :, :, :, cols] = r.reshape(ZH, ZL, YS, CS, rows, group)

        loop(3, tile)

    def grad_x(g):
        before = h2 if g == 0 else n1
        n1[...] = before[...] + dot(qkv[g], weight(g), NT)
        if g == 2:
            store_x.append(store(n1, gtok_hbm.at[0], 2))

    last = len(SUMMED) - 1
    every = (ALL, ALL)
    mine = (zh, zl)

    def at_z(zz):
        return (zz // ZL, lax.rem(zz, ZL))

    def gpiece(k, zi, yy, cc, cols=ALL):
        if k < 4:
            return gd.at[(k, *zi, yy, cc, ALL, cols)]
        if k < 8:
            return wd.at[(*zi, yy, cc, k - 4, ALL, cols)]
        if k < 9:
            return go.at[(0, *zi, yy, cc, ALL, cols)]
        return wa.at[(IN + k - 9, *zi, yy, cc, ALL, cols)]

    def left(i):
        return pl.ds(SUMMED[i][1], SUMMED[i][2])

    def right(i):
        return pl.ds(half + SUMMED[i][1], SUMMED[i][2])

    def near(i):
        return left(i)

    def both(i):
        return (ALL,) if SUMMED[i][2] == half else (left(i), right(i))

    def r_core(i, cols):
        k = SUMMED[i][0]
        return remote(
            gpiece(k, every, ALL, 1 - c, cols), rcore.at[k % RING, :, :, :, :, cols], r_sent.at[i], rrc.at[i], sibling
        )

    def r_ya(i):
        k = SUMMED[i][0]
        src, dst = gpiece(k, every, 1 - y, c, left(i)), rya.at[k, :, :, :, near(i)]
        return remote(src, dst, r_sent.at[i], rry.at[i, 0], across_y)

    def r_xb(i):
        k = SUMMED[i][0]
        src, dst = gpiece(k, (ALL, 1 - parity(i)), ALL, c, right(i)), rxb.at[k, :, :, :, near(i)]
        return remote(src, dst, r_sent.at[i], rrx.at[i, 0], across_x)

    def r_za(i, dz):
        k = SUMMED[i][0]
        src, dst = gpiece(k, at_z(ahead(dz)), y, c, left(i)), rza.at[k, dz - 1, :, near(i)]
        return remote(src, dst, r_sent.at[i], rrz.at[i, 0], device(ahead(dz), y, c, px))

    def r_yb(i):
        k = SUMMED[i][0]
        src, dst = gpiece(k, (ALL, parity(i)), 1 - y, c, right(i)), ryb.at[k, :, :, near(i)]
        return remote(src, dst, r_sent.at[i], rry.at[i, 1], across_y)

    def r_xa(i):
        k = SUMMED[i][0]
        src, dst = gpiece(k, mine, y, c, left(i)), rxa.at[k, :, near(i)]
        return remote(src, dst, r_sent.at[i], rrx.at[i, 1], across_x)

    def r_zb(i, dz):
        k = SUMMED[i][0]
        src, dst = gpiece(k, at_z(ahead(dz)), y, c, right(i)), rzb.at[k, dz - 1, :, near(i)]
        return remote(src, dst, r_sent.at[i], rrz.at[i, 1], device(ahead(dz), y, c, px))

    def r_fb(i):
        k = SUMMED[i][0]
        return remote(
            gpiece(k, mine, y, c, right(i)), rfb.at[k, :, near(i)], r_sent.at[i], rrf.at[i], across_x
        )

    v_rc = remote(gv.at[:, :, :, 1 - c], rv_core, rv_sent, wrc, sibling)
    v_ry = remote(gv.at[:, :, 1 - y, c], rv_y, rv_sent, wry, across_y)
    v_rx = remote(gv.at[(*mine, y, c)], rv_x, rv_sent, wrx, across_x)

    def v_rz(dz):
        where = device(ahead(dz), y, c, px)
        return remote(gv.at[(*at_z(ahead(dz)), y, c)], rv_z.at[dz - 1], rv_sent, wrz, where)

    def parity(i):
        return lax.rem(px + i, 2)

    def same(i):
        return zl == parity(i)


    def add_into(ref, *others):
        if len(others) == 1:
            ref[...] += others[0][...]
            return
        total = ref[...].astype(F32)
        for other in others:
            total = total + other[...].astype(F32)
        ref[...] = total.astype(BF)

    def r0(i):
        for cols in both(i):
            r_core(i, cols).start()
        if i == last:
            v_rc.start()

    def r1(i):
        k, _, width = SUMMED[i]
        drained(wa.at[0, :, :, :, 0, :, pl.ds(0, 2 * width)], rrc.at[i])

        def add(zz):
            for cols in both(i):
                add_into(gpiece(k, at_z(zz), ALL, c, cols), rcore.at[(k % RING, *at_z(zz), ALL, ALL, cols)])

        loop(ZS, add)
        r_ya(i).start()
        r_xb(i).start()
        if i == last:
            v_rc.wait_recv()
            add_into(gv.at[:, :, :, c], rv_core)
            v_ry.start()

    def r2a(i):
        k = SUMMED[i][0]
        r_ya(i).wait_recv()
        add_into(gpiece(k, every, y, c, left(i)), rya.at[k, :, :, :, near(i)])
        for dz in (1, 2, 3):
            r_za(i, dz).start()
        if i == last:
            v_ry.wait_recv()
            add_into(gv.at[:, :, y, c], rv_y)
            for dz in (1, 2, 3):
                v_rz(dz).start()

    def r2b(i):
        k = SUMMED[i][0]
        r_xb(i).wait_recv()
        add_into(gpiece(k, (ALL, parity(i)), ALL, c, right(i)), rxb.at[k, :, :, :, near(i)])
        r_yb(i).start()

    def r3a(i):
        k = SUMMED[i][0]
        drained(rza.at[k, :, :, near(i)], rrz.at[i, 0])
        add_into(gpiece(k, mine, y, c, left(i)), *(rza.at[k, dz, :, near(i)] for dz in range(3)))
        r_xa(i).start()
        if i == last:
            drained(rv_z, wrz)
            add_into(gv.at[(*mine, y, c)], rv_z.at[0], rv_z.at[1], rv_z.at[2])
            v_rx.start()

    def r3b(i):
        k = SUMMED[i][0]
        r_yb(i).wait_recv()
        add_into(gpiece(k, (ALL, parity(i)), y, c, right(i)), ryb.at[k, :, :, near(i)])
        pl.when(same(i))(lambda: r_zb(i, 2).start())

        @pl.when(jnp.logical_not(same(i)))
        def _():
            r_zb(i, 1).start()
            r_zb(i, 3).start()

    def r4a(i):
        k = SUMMED[i][0]
        r_xa(i).wait_recv()
        fin[k, :, left(i)] = gpiece(k, mine, y, c, left(i))[...].astype(F32) + rxa[k, :, near(i)].astype(F32)
        if i == last:
            v_rx.wait_recv()
            store_vec.append(store(gv.at[(*mine, y, c)], gvec_hbm.at[0], 3))
            store_vec.append(store(rv_x, gvec_hbm.at[1], 4))
        settle(k)

    def r4b(i):
        k = SUMMED[i][0]

        @pl.when(same(i))
        def _():
            drained(rzb.at[k, :, :, near(i)], rrz.at[i, 1])
            piece = gpiece(k, mine, y, c, right(i))
            add_into(piece, *(rzb.at[k, dz, :, near(i)] for dz in range(3)))
            r_fb(i).start()
            fin[k, :, right(i)] = piece[...].astype(F32)

    def r5(i):
        k = SUMMED[i][0]

        @pl.when(jnp.logical_not(same(i)))
        def _():
            r_fb(i).wait_recv()
            fin[k, :, right(i)] = rfb[k, :, near(i)].astype(F32)

        settle(k)

    store_out, store_x, store_vec = [], [], []
    open_ends = {k: 2 * sum(part[0] == k for part in SUMMED) for k in range(CHUNKS)}

    def store(src, dst, i=0):
        cp = pltpu.make_async_copy(src, dst, s_store.at[i])
        cp.start()
        return cp

    def settle(k):
        open_ends[k] -= 1
        if open_ends[k]:
            return
        if k < 4:
            store(fin.at[k], gdown_hbm.at[pl.ds(k * rows, rows)])
        elif k < 8:
            store(fin.at[k], gin_hbm.at[:, pl.ds((k - 4) * model, model)])
        elif k < 9:
            store(fin.at[k], gout_hbm)
        else:
            for part in range(3):
                store(
                    fin.at[k, :, pl.ds(part * group, group)],
                    gqkv_hbm.at[:, pl.ds(part * model + (k - 9) * group, group)],
                )

    steps = (
        e1, eo, e2, e3, e4, e5,
        r0, r1, r2a, r2b, r3a, r3b,
        r4a, r4b, r5, spread_params, project, attend,
        out_proj, feed_up, feed_down, norm_two, grad_down, grad_act,
        grad_in, grad_normed, norm_one_back, grad_out, grad_context, attend_back,
        grad_qkv, gather_grads, grad_x,
    )
    vg[...] = jnp.zeros_like(vg)
    for step, i in ORDER:
        if step == S_PROJECT and i == 0:
            load_x.wait()
        if step == S_NORM2:
            load_cot.wait()
        steps[step](i)
    sent(*range(IN))
    vec_sent()
    for i, (_, _, width) in enumerate(SUMMED):
        drained(wa.at[0, :, :, :, :, :, pl.ds(0, 2 * width)], r_sent.at[i])
    drained(gv, rv_sent)
    drained(fin, s_store.at[0])
    for cp in (*store_vec, *store_x):
        cp.wait()


def place_kernel(cuts, *refs):
    count = len(cuts)
    sources, targets, held = refs[: count + 1], refs[count + 1 : 2 * count + 2], refs[2 * count + 2 : 3 * count + 3]
    vector, sem_in, sem_out = refs[3 * count + 3 :]
    first = pltpu.make_async_copy(sources[count], held[count], sem_in.at[sum(cuts)])
    first.start()
    moves = []
    for src, dst, mid, parts in zip(sources, targets, held, cuts):
        size = src.shape[-2] // parts
        for j in range(parts):
            at = (slice(None),) * (len(src.shape) - 2) + (pl.ds(j * size, size),)
            i = len(moves)
            moves.append(
                (
                    pltpu.make_async_copy(src.at[at], mid.at[at], sem_in.at[i]),
                    pltpu.make_async_copy(mid.at[at], dst.at[at], sem_out.at[i]),
                )
            )
    for into, _ in moves:
        into.start()
    first.wait()
    segment = vector.shape[0] // 3
    total = held[count][0].astype(F32) + held[count][1].astype(F32)
    vector[...] = jnp.concatenate([total[s : s + 1, 0:segment] for s in range(3)], axis=1).reshape(-1)
    last = pltpu.make_async_copy(vector, targets[count], sem_out.at[sum(cuts)])
    last.start()
    for into, out in moves:
        into.wait()
        out.start()
    for _, out in moves:
        out.wait()
    last.wait()


def fused_layer(tokens, lengths, w_qkv, w_out, w_in, w_down, norms_biases, cotangent):
    seq, model = tokens.shape[1:]
    rows = w_qkv.shape[0]
    hidden = w_in.shape[1]
    half = model // 2
    group = model // 3
    vm, dma = pltpu.VMEM, pltpu.SemaphoreType.DMA
    grid = (ZH, ZL, YS, CS)
    n, m, u = CHUNKS, len(GATHERED), len(SUMMED)
    scratch = [
        vm((DOWN, *grid, rows, model), BF),
        vm((*grid, 4, rows, model), BF),
        vm((*grid, 16, 256), BF),
        vm((4, *grid, rows, model), BF),
        vm((1, *grid, rows, model), BF),
        vm((*grid, 16, 256), BF),
        vm((RING, ZH, ZL, YS, rows, model), BF),
        vm((n, ZH, ZL, rows, half), BF),
        vm((n, ZH, YS, rows, half), BF),
        vm((n, 3, rows, half), BF),
        vm((n, ZH, rows, half), BF),
        vm((n, 3, rows, half), BF),
        vm((n, rows, half), BF),
        vm((n, rows, half), BF),
        vm((ZH, ZL, YS, 16, 256), BF),
        vm((ZH, ZL, 16, 256), BF),
        vm((3, 16, 256), BF),
        vm((16, 256), BF),
        vm((n, rows, model), F32),
        vm(norms_biases.shape, BF),
        vm((seq, model), BF),
        vm((seq, model), BF),
        vm((3, seq, model), BF),
        vm((model, seq), BF),
        vm((3, group // (model // HEADS), seq, seq), BF),
        vm((model, seq), BF),
        vm((seq, model), F32),
        vm((seq, model), BF),
        vm((model, seq), BF),
        vm((ZS * YS, CS, 4, rows, seq), BF),
        vm((seq, hidden), BF),
        vm((seq, model), F32),
        vm((seq, model), BF),
        vm((seq, model), BF),
        vm((seq, 1), F32),
        vm((16, model), F32),
        vm((16, model), F32),
        dma((n,)), dma((3,)), dma((5,)),
        dma((m,)), dma((m,)), dma((m,)), dma((m,)), dma((m,)), dma, dma, dma, dma,
        dma((u,)), dma, dma((u,)), dma((u, 2)), dma((u, 2)), dma((u, 2)), dma((u,)), dma, dma, dma, dma,
    ]
    hbm = pl.BlockSpec(memory_space=pl.ANY)
    shape = jax.ShapeDtypeStruct
    outs = pl.pallas_call(
        layer_kernel,
        out_shape=(
            shape(tokens.shape, BF),
            shape(tokens.shape, F32),
            shape(w_qkv.shape, F32),
            shape(w_out.shape, F32),
            shape(w_in.shape, F32),
            shape(w_down.shape, F32),
            shape((2, 16, 256), BF),
        ),
        in_specs=[hbm, pl.BlockSpec(memory_space=pltpu.SMEM)] + [hbm] * 6,
        out_specs=(hbm,) * 7,
        scratch_shapes=scratch,
        compiler_params=pltpu.CompilerParams(
            collective_id=0, has_side_effects=True, vmem_limit_bytes=64 << 20
        ),
        name="layer",
    )(tokens, lengths, w_qkv, w_out, w_in, w_down, norms_biases, cotangent)
    cuts = (1, 2, 1, 1, 1, 1)
    *placed, grad_vector = pl.pallas_call(
        functools.partial(place_kernel, cuts),
        out_shape=(*(shape(o.shape, o.dtype) for o in outs[:6]), shape(norms_biases.shape, F32)),
        in_specs=[hbm] * 7,
        out_specs=(hbm,) * 7,
        scratch_shapes=[vm(o.shape, o.dtype) for o in outs]
        + [vm(norms_biases.shape, F32), dma((sum(cuts) + 1,)), dma((sum(cuts) + 1,))],
        name="place",
    )(*outs)
    return (*placed, grad_vector)


def norm_rows(values, gain_row, shift_row):
    average = jnp.mean(values, -1, keepdims=True)
    centred = values - average
    spread = jnp.mean(centred * centred, -1, keepdims=True)
    return centred * lax.rsqrt(spread + 1e-06) * gain_row + shift_row


def gelu_exact(values):
    return jax.nn.gelu(values, approximate=False)


def column_sum(values):
    return jnp.sum(values.astype(jnp.float32), 0)


def split_vector(vector, model_width, hidden_width):
    segments = [
        vector[position * model_width : (position + 1) * model_width] for position in range(8)
    ]
    return segments + [vector[8 * model_width : 8 * model_width + hidden_width]]


def pair_blocks(projected, head_count):
    row_count = projected.shape[0]
    pair_count = head_count // 2
    pair_width = projected.shape[1] // (3 * pair_count)
    return projected.reshape(row_count, 3, pair_count, pair_width).transpose(2, 1, 0, 3)


def unpair_blocks(blocks):
    pair_count = blocks.shape[0]
    row_count = blocks.shape[2]
    pair_width = blocks.shape[3]
    return blocks.transpose(2, 1, 0, 3).reshape(row_count, 3 * pair_count * pair_width)


def pair_scores(head_block, usable, factor):
    row_count = head_block.shape[1]
    queries = head_block[0].reshape(row_count, 2, -1)
    key_rows = head_block[1].reshape(row_count, 2, -1)
    values = head_block[2].reshape(row_count, 2, -1)
    scores = (
        jnp.einsum("qhd,khd->hqk", queries, key_rows, preferred_element_type=jnp.float32) * factor
    )
    return (queries, key_rows, values, jnp.where(usable[None, None, :], scores, -1000000000.0))


def attention_forward(blocks, usable, factor):

    def one_pair(head_block):
        queries, key_rows, values, scores = pair_scores(head_block, usable, factor)
        highest = jnp.max(scores, -1, keepdims=True)
        raised = jnp.exp(scores - highest)
        summed = jnp.sum(raised, -1, keepdims=True)
        attend = (raised / summed).astype(jnp.bfloat16)
        context = jnp.einsum("hqk,khd->qhd", attend, values, preferred_element_type=jnp.float32)
        return (context.reshape(context.shape[0], -1), highest[..., 0] + jnp.log(summed[..., 0]))

    return lax.map(one_pair, blocks)


def attention_backward(blocks, grad_pairs, log_totals, usable, factor):

    def one_pair(pair_inputs):
        head_block, grad_context, log_total = pair_inputs
        queries, key_rows, values, scores = pair_scores(head_block, usable, factor)
        attend = jnp.exp(scores - log_total[..., None])
        row_count = grad_context.shape[0]
        grad_heads = grad_context.reshape(row_count, 2, -1)
        grad_values = jnp.einsum(
            "hqk,qhd->khd",
            attend.astype(jnp.bfloat16),
            grad_heads,
            preferred_element_type=jnp.float32,
        )
        grad_attend = jnp.einsum(
            "qhd,khd->hqk", grad_heads, values, preferred_element_type=jnp.float32
        )
        grad_scores = attend * (grad_attend - jnp.sum(attend * grad_attend, -1, keepdims=True))
        grad_low = grad_scores.astype(jnp.bfloat16)
        grad_queries = (
            jnp.einsum("hqk,khd->qhd", grad_low, key_rows, preferred_element_type=jnp.float32)
            * factor
        )
        grad_keys = (
            jnp.einsum("hqk,qhd->khd", grad_low, queries, preferred_element_type=jnp.float32)
            * factor
        )
        return jnp.stack(
            [
                grad_queries.reshape(row_count, -1),
                grad_keys.reshape(row_count, -1),
                grad_values.reshape(row_count, -1),
            ]
        )

    return lax.map(one_pair, (blocks, grad_pairs, log_totals))


def layer_forward(inputs, length, weights):
    w_qkv, w_out, w_in, w_down, vector = weights
    row_count, model_width = inputs.shape
    hidden_width = w_in.shape[1]
    params = split_vector(vector.astype(jnp.float32), model_width, hidden_width)
    joined_bias = jnp.concatenate([params[0], jnp.zeros((model_width,), jnp.float32), params[1]])
    projected = (jnp.dot(inputs, w_qkv, preferred_element_type=jnp.float32) + joined_bias).astype(
        jnp.bfloat16
    )
    blocks = pair_blocks(projected, HEADS)
    usable = jnp.arange(row_count) < length
    factor = (model_width // HEADS) ** (-0.5)
    context_pairs, log_totals = attention_forward(blocks, usable, factor)
    context = context_pairs.transpose(1, 0, 2).reshape(row_count, model_width).astype(jnp.bfloat16)
    resid_one = inputs.astype(jnp.float32) + (
        jnp.dot(context, w_out, preferred_element_type=jnp.float32) + params[2]
    )
    normed_one = norm_rows(resid_one, params[3], params[4])
    normed_low = normed_one.astype(jnp.bfloat16)
    pre_act = jnp.dot(normed_low, w_in, preferred_element_type=jnp.float32) + params[8]
    activated = gelu_exact(pre_act).astype(jnp.bfloat16)
    resid_two = normed_one + (
        jnp.dot(activated, w_down, preferred_element_type=jnp.float32) + params[5]
    )
    result = norm_rows(resid_two, params[6], params[7])
    saved = (
        params,
        blocks,
        usable,
        factor,
        log_totals,
        context,
        resid_one,
        normed_low,
        pre_act,
        activated,
        resid_two,
    )
    return (result, saved)


def layer_backward(inputs, length, grad_result, weights):
    w_qkv, w_out, w_in, w_down, vector = weights
    unused_result, saved = layer_forward(inputs, length, weights)
    (
        params,
        blocks,
        usable,
        factor,
        log_totals,
        context,
        resid_one,
        normed_low,
        pre_act,
        activated,
        resid_two,
    ) = saved
    row_count, model_width = inputs.shape
    unused_two, norm_two_back = jax.vjp(norm_rows, resid_two, params[6], params[7])
    grad_two, grad_gain_two, grad_shift_two = norm_two_back(grad_result)
    grad_feed = grad_two.astype(jnp.bfloat16)
    grad_down = jnp.einsum("sf,sd->fd", activated, grad_feed, preferred_element_type=jnp.float32)
    grad_act = jnp.einsum("sd,fd->sf", grad_feed, w_down, preferred_element_type=jnp.float32)
    unused_act, gelu_back = jax.vjp(gelu_exact, pre_act)
    grad_pre = gelu_back(grad_act)[0].astype(jnp.bfloat16)
    grad_in = jnp.einsum("sd,sf->df", normed_low, grad_pre, preferred_element_type=jnp.float32)
    grad_normed = grad_two + jnp.einsum(
        "sf,df->sd", grad_pre, w_in, preferred_element_type=jnp.float32
    )
    unused_one, norm_one_back = jax.vjp(norm_rows, resid_one, params[3], params[4])
    grad_one, grad_gain_one, grad_shift_one = norm_one_back(grad_normed)
    grad_attended = grad_one.astype(jnp.bfloat16)
    grad_out = jnp.einsum("sd,se->de", context, grad_attended, preferred_element_type=jnp.float32)
    grad_context = jnp.einsum(
        "se,de->sd", grad_attended, w_out, preferred_element_type=jnp.float32
    ).astype(jnp.bfloat16)
    grad_pairs = grad_context.reshape(row_count, HEADS // 2, -1).transpose(1, 0, 2)
    grad_blocks = attention_backward(blocks, grad_pairs, log_totals, usable, factor)
    grad_projected = unpair_blocks(grad_blocks).astype(jnp.bfloat16)
    grad_qkv = jnp.einsum("sd,se->de", inputs, grad_projected, preferred_element_type=jnp.float32)
    grad_inputs = grad_one + jnp.einsum(
        "se,de->sd", grad_projected, w_qkv, preferred_element_type=jnp.float32
    )
    projected_sums = column_sum(grad_projected)
    grad_vector = jnp.concatenate(
        [
            projected_sums[:model_width],
            projected_sums[2 * model_width :],
            column_sum(grad_attended),
            grad_gain_one,
            grad_shift_one,
            column_sum(grad_feed),
            grad_gain_two,
            grad_shift_two,
            column_sum(grad_pre),
        ]
    )
    return (grad_inputs, (grad_qkv, grad_out, grad_in, grad_down, grad_vector))


def local(tokens, lengths, w_qkv, w_out, w_in, w_down, norms_biases, cotangent):
    weights = (
        lax.all_gather(w_qkv, "wide", axis=0, tiled=True),
        lax.all_gather(w_out, "wide", axis=0, tiled=True),
        lax.all_gather(w_in, "wide", axis=0, tiled=True),
        lax.all_gather(w_down, "wide", axis=0, tiled=True),
        lax.all_gather(norms_biases, "wide", axis=0, tiled=True),
    )

    def forward_one(sequence):
        return layer_forward(sequence[0], sequence[1], weights)[0].astype(jnp.bfloat16)

    output = lax.map(forward_one, (tokens, lengths))
    second_copy = (
        lax.all_gather(w_qkv, "wide", axis=0, tiled=True),
        lax.all_gather(w_out, "wide", axis=0, tiled=True),
        lax.all_gather(w_in, "wide", axis=0, tiled=True),
        lax.all_gather(w_down, "wide", axis=0, tiled=True),
        lax.all_gather(norms_biases, "wide", axis=0, tiled=True),
    )
    running = tuple((jnp.zeros(member.shape, jnp.float32) for member in second_copy))

    def advance(totals, sequence):
        grad_inputs, gradients = layer_backward(
            sequence[0], sequence[1], sequence[2].astype(jnp.float32), second_copy
        )
        return (jax.tree.map(jnp.add, totals, gradients), grad_inputs)

    totals, grad_tokens = lax.scan(advance, running, (tokens, lengths, cotangent))
    owned_rows = (
        lax.psum_scatter(
            totals[0].astype(jnp.bfloat16), "wide", scatter_dimension=0, tiled=True
        ).astype(jnp.float32),
        lax.psum_scatter(
            totals[1].astype(jnp.bfloat16), "wide", scatter_dimension=0, tiled=True
        ).astype(jnp.float32),
        lax.psum_scatter(
            totals[2].astype(jnp.bfloat16), "wide", scatter_dimension=0, tiled=True
        ).astype(jnp.float32),
        lax.psum_scatter(
            totals[3].astype(jnp.bfloat16), "wide", scatter_dimension=0, tiled=True
        ).astype(jnp.float32),
        lax.psum_scatter(
            totals[4].astype(jnp.bfloat16), "wide", scatter_dimension=0, tiled=True
        ).astype(jnp.float32),
    )
    summed_all = (
        lax.psum(owned_rows[0].astype(jnp.bfloat16), "narrow").astype(jnp.float32),
        lax.psum(owned_rows[1].astype(jnp.bfloat16), "narrow").astype(jnp.float32),
        lax.psum(owned_rows[2].astype(jnp.bfloat16), "narrow").astype(jnp.float32),
        lax.psum(owned_rows[3].astype(jnp.bfloat16), "narrow").astype(jnp.float32),
        lax.psum(owned_rows[4].astype(jnp.bfloat16), "narrow").astype(jnp.float32),
    )
    return (
        output,
        grad_tokens,
        summed_all[0],
        summed_all[1],
        summed_all[2],
        summed_all[3],
        summed_all[4],
    )


def solution(mesh):
    in_specs = (
        P(("wide", "narrow"), None, None),
        P(("wide", "narrow")),
        P("wide", None),
        P("wide", None),
        P("wide", None),
        P("wide", None),
        P("wide"),
        P(("wide", "narrow"), None, None),
    )
    out_specs = (
        P(("wide", "narrow"), None, None),
        P(("wide", "narrow"), None, None),
        P("wide", None),
        P("wide", None),
        P("wide", None),
        P("wide", None),
        P("wide"),
    )
    chips = (ZS * YS * CS, 2)
    fused = tuple(mesh.shape[axis] for axis in ("wide", "narrow")) == chips
    step = fused_layer if fused else local
    return jax.shard_map(step, mesh=mesh, in_specs=in_specs, out_specs=out_specs, check_vma=False)
```

profile of v0, /device:TPU:0, one launch (start us, length us, event | category | flops | bytes accessed | tf_op | source)
XLA Modules:
  0.0 152.4 jit_solution(11621818435686833461)
XLA Ops:
  1.3 147.6 %layer.1 = (bf16[1,512,768]{2,1,0:T(8,128)(2,1)}, f32[1,512,768]{2,1,0:T(8,128)}, f32[48,2304]{1,0:T(8,128)}, f32[48,768]{1,0:T(8,128)}, f32[48,3072]{1,0:T(8,12...) custom-call(bf16[1,512,768]{2,1,0:T(8,128)(2,1)} %x_hbm.1, s32[1]{0:T(128)S(6)} %copy.15.len_ref, ...), custom_call_target="tpu_custom_call" | custom-call | tf_op jit(solution)/shard_map/layer/pallas_call | solution.py:833
  148.8 3.3 %place.1 = (bf16[1,512,768]{2,1,0:T(8,128)(2,1)}, f32[1,512,768]{2,1,0:T(8,128)}, f32[48,2304]{1,0:T(8,128)}, f32[48,768]{1,0:T(8,128)}, f32[48,3072]{1,0:T(8,128)}, /*index=5*/f32[192,768]{1,0:T(8,128)}, f32[576]{0:T(1024)}) custom-call(bf16[1,512,768]{2,1,0:T(8,128)(2,1)} %get-tuple-element.14.refs_0_, f32[1,512,768]{2,1,0:T(8,128)} %get-tuple-element.15.refs_1_, ...), custom_call_target="tpu_custom_call" | custom-call | tf_op jit(solution)/shard_map/place/pallas_call | solution.py:853
where the time goes:
time: 153 us; the launch traced here: 152 us
  Pallas kernels  151 us (99%)
    pallas_call x1, Pallas kernels, fused_layer(): pl.pallas_call(layer_kernel, out_shape=(shape(tokens.shape, BF), shape(to...  148 us
    pallas_call x1, Pallas kernels, fused_layer(): pl.pallas_call(functools.partial(place_kernel, cuts), out_shape=(*(shape(...  3.34 us

commit v1 on v0

--- a/solution.py
+++ b/solution.py
@@ -29,40 +29,42 @@
     (8, 0, 384), (8, 384, 384), (9, 0, 384), (9, 384, 384), (10, 0, 384), (10, 384, 384), (11, 0, 384), (11, 384, 384),
 )
 SUMMED = (
-    (0, 0, 384), (1, 0, 384), (2, 0, 384), (3, 0, 384), (4, 0, 384), (5, 0, 384), (6, 0, 384), (7, 0, 384),
-    (8, 0, 384), (9, 0, 384), (10, 0, 384), (11, 0, 384),
+    (0, 0, 128), (0, 128, 128), (0, 256, 128), (1, 0, 384), (2, 0, 384), (3, 0, 384), (4, 0, 384), (5, 0, 384),
+    (6, 0, 384), (7, 0, 384), (8, 0, 384), (9, 0, 384), (10, 0, 384), (11, 0, 384),
 )
 ORDER = (
-    (S_EO, 0), (S_E1, 0), (S_EO, 1), (S_E1, 1), (S_E1, 2), (S_EO, 2), (S_EO, 3), (S_E1, 3), (S_EO, 4), (S_EO, 5),
-    (S_E2, 0), (S_E1, 4), (S_EO, 6), (S_E2, 1), (S_E1, 5), (S_EO, 7), (S_E3, 0), (S_E2, 2), (S_E1, 6), (S_EO, 8),
-    (S_E3, 1), (S_E2, 3), (S_E4, 0), (S_E1, 7), (S_EO, 9), (S_E5, 0), (S_E3, 2), (S_E2, 4), (S_E4, 1), (S_E1, 8),
-    (S_EO, 10), (S_E5, 1), (S_E3, 3), (S_SPREAD, 0), (S_E4, 2), (S_E2, 5), (S_E1, 9), (S_EO, 11), (S_PROJECT, 0), (S_E5, 2),
-    (S_E3, 4), (S_E4, 3), (S_E2, 6), (S_E1, 10), (S_EO, 12), (S_ATTEND, 0), (S_E5, 3), (S_E4, 4), (S_E3, 5), (S_E3, 6),
-    (S_E2, 7), (S_E2, 8), (S_E1, 11), (S_E1, 12), (S_E5, 4), (S_EO, 13), (S_EO, 14), (S_PROJECT, 1), (S_E2, 9), (S_E4, 5),
-    (S_E1, 13), (S_EO, 15), (S_ATTEND, 1), (S_E5, 5), (S_E4, 6), (S_E3, 7), (S_E3, 8), (S_E2, 10), (S_E1, 14), (S_E2, 11),
-    (S_E1, 15), (S_E5, 6), (S_EO, 16), (S_EO, 17), (S_PROJECT, 2), (S_E3, 9), (S_E4, 7), (S_E2, 12), (S_E1, 16), (S_EO, 18),
-    (S_ATTEND, 2), (S_E5, 7), (S_E4, 8), (S_E4, 9), (S_E3, 10), (S_E3, 11), (S_E2, 13), (S_E2, 14), (S_E1, 17), (S_E5, 8),
-    (S_E1, 18), (S_E5, 9), (S_E3, 12), (S_EO, 19), (S_EO, 20), (S_OUT, 0), (S_E4, 10), (S_E3, 13), (S_E4, 11), (S_E2, 15),
-    (S_E2, 16), (S_E5, 10), (S_E1, 19), (S_E1, 20), (S_E5, 11), (S_E3, 14), (S_EO, 21), (S_EO, 22), (S_UP, 0), (S_E4, 12),
-    (S_E2, 17), (S_E4, 13), (S_E3, 15), (S_E1, 21), (S_E5, 12), (S_E2, 18), (S_E5, 13), (S_E1, 22), (S_EO, 23), (S_UP, 1),
-    (S_E4, 14), (S_E3, 16), (S_E2, 19), (S_E1, 23), (S_UP, 2), (S_E5, 14), (S_E4, 15), (S_E3, 17), (S_E2, 20), (S_E3, 18),
-    (S_E4, 16), (S_E5, 15), (S_UP, 3), (S_E5, 16), (S_E4, 17), (S_E3, 19), (S_E2, 21), (S_E2, 22), (S_E5, 17), (S_E3, 20),
-    (S_E4, 18), (S_DOWN, 0), (S_E4, 19), (S_E5, 18), (S_E2, 23), (S_E3, 21), (S_E5, 19), (S_DOWN, 1), (S_E3, 22), (S_E4, 20),
-    (S_E3, 23), (S_E5, 20), (S_E4, 21), (S_E4, 22), (S_E5, 21), (S_DOWN, 2), (S_E5, 22), (S_E4, 23), (S_E5, 23), (S_DOWN, 3),
-    (S_NORM2, 0), (S_GDOWN, 0), (S_R0, 0), (S_GDOWN, 1), (S_GACT, 0), (S_R1, 0), (S_R0, 1), (S_GDOWN, 2), (S_GDOWN, 3), (S_R0, 2),
-    (S_R0, 3), (S_R1, 1), (S_GACT, 1), (S_GACT, 2), (S_GACT, 3), (S_R2A, 0), (S_R1, 3), (S_GNORM, 0), (S_R1, 2), (S_GIN, 0),
-    (S_R2A, 1), (S_GIN, 1), (S_R2B, 1), (S_R2B, 0), (S_R0, 4), (S_GNORM, 1), (S_R2A, 3), (S_GIN, 2), (S_GIN, 3), (S_R2B, 3),
-    (S_R0, 5), (S_R2A, 2), (S_GNORM, 2), (S_GNORM, 3), (S_R0, 6), (S_R0, 7), (S_R1, 4), (S_R3B, 1), (S_NORM1, 0), (S_GOUT, 0),
-    (S_R1, 6), (S_R3B, 0), (S_R0, 8), (S_R3B, 3), (S_R1, 5), (S_GCTX, 0), (S_R3A, 3), (S_R1, 8), (S_R2A, 4), (S_ABACK, 0),
-    (S_R2A, 6), (S_ABACK, 1), (S_R2A, 5), (S_R1, 7), (S_R2B, 2), (S_GQKV, 0), (S_R2B, 5), (S_R3A, 2), (S_R4B, 3), (S_R2A, 8),
-    (S_ABACK, 2), (S_R2A, 7), (S_R0, 9), (S_R2B, 4), (S_GQKV, 1), (S_R3B, 2), (S_R2B, 7), (S_R2B, 8), (S_GQKV, 2), (S_R1, 9),
-    (S_R2B, 6), (S_R3B, 5), (S_R3A, 5), (S_GX, 0), (S_R0, 10), (S_R3A, 1), (S_R4A, 3), (S_R3B, 4), (S_GGRADS, 0), (S_R4B, 0),
-    (S_R3A, 8), (S_R3B, 8), (S_R0, 11), (S_R3B, 7), (S_GX, 1), (S_R2B, 9), (S_R1, 11), (S_R2A, 9), (S_R3B, 6), (S_R5, 0),
-    (S_R1, 10), (S_R3A, 6), (S_GX, 2), (S_R3A, 7), (S_R3B, 9), (S_R4B, 7), (S_R2A, 11), (S_R2B, 11), (S_R5, 3), (S_R3A, 4),
-    (S_R4B, 8), (S_R4A, 2), (S_R4A, 1), (S_R4B, 1), (S_R3A, 0), (S_R4B, 5), (S_R2B, 10), (S_R2A, 10), (S_R4B, 4), (S_R3A, 9),
-    (S_R4B, 2), (S_R3B, 11), (S_R4A, 5), (S_R4B, 9), (S_R5, 1), (S_R4A, 0), (S_R4A, 7), (S_R3B, 10), (S_R4A, 4), (S_R3A, 11),
-    (S_R5, 9), (S_R3A, 10), (S_R4A, 8), (S_R4A, 9), (S_R4B, 6), (S_R5, 4), (S_R4A, 11), (S_R5, 7), (S_R4B, 11), (S_R5, 2),
-    (S_R5, 6), (S_R5, 8), (S_R4B, 10), (S_R4A, 10), (S_R5, 5), (S_R4A, 6), (S_R5, 11), (S_R5, 10),
+    (S_E1, 0), (S_EO, 0), (S_E1, 1), (S_EO, 1), (S_E1, 2), (S_EO, 2), (S_EO, 3), (S_EO, 4), (S_EO, 5), (S_E1, 3),
+    (S_E2, 0), (S_EO, 6), (S_E1, 4), (S_E2, 1), (S_EO, 7), (S_E1, 5), (S_E2, 2), (S_EO, 8), (S_E3, 0), (S_E1, 6),
+    (S_E2, 3), (S_EO, 9), (S_E3, 1), (S_E1, 7), (S_E2, 4), (S_EO, 10), (S_E3, 2), (S_E4, 0), (S_E1, 8), (S_E2, 5),
+    (S_EO, 11), (S_E3, 3), (S_E4, 1), (S_E5, 0), (S_E1, 9), (S_E2, 6), (S_EO, 12), (S_E3, 4), (S_E4, 2), (S_E5, 1),
+    (S_SPREAD, 0), (S_PROJECT, 0), (S_E1, 10), (S_E2, 7), (S_EO, 13), (S_E3, 5), (S_E4, 3), (S_E5, 2), (S_ATTEND, 0), (S_E1, 11),
+    (S_E2, 8), (S_EO, 14), (S_E3, 6), (S_E4, 4), (S_E5, 3), (S_ATTEND, 1), (S_E1, 12), (S_E2, 9), (S_EO, 15), (S_E3, 7),
+    (S_E4, 5), (S_E5, 4), (S_PROJECT, 1), (S_E1, 13), (S_E2, 10), (S_EO, 16), (S_E3, 8), (S_E4, 6), (S_E5, 5), (S_ATTEND, 2),
+    (S_E1, 14), (S_E2, 11), (S_EO, 17), (S_E3, 9), (S_E4, 7), (S_E5, 6), (S_ATTEND, 3), (S_E1, 15), (S_E2, 12), (S_EO, 18),
+    (S_E3, 10), (S_E4, 8), (S_E5, 7), (S_PROJECT, 2), (S_E1, 16), (S_E2, 13), (S_EO, 19), (S_E3, 11), (S_E4, 9), (S_E5, 8),
+    (S_ATTEND, 4), (S_E1, 17), (S_E2, 14), (S_EO, 20), (S_E3, 12), (S_E4, 10), (S_E5, 9), (S_ATTEND, 5), (S_E1, 18), (S_E2, 15),
+    (S_EO, 21), (S_E3, 13), (S_E4, 11), (S_E5, 10), (S_OUT, 0), (S_E1, 19), (S_E2, 16), (S_EO, 22), (S_E3, 14), (S_E4, 12),
+    (S_E5, 11), (S_UP, 0), (S_E1, 20), (S_E2, 17), (S_EO, 23), (S_E3, 15), (S_E4, 13), (S_E5, 12), (S_UP, 1), (S_E1, 21),
+    (S_E2, 18), (S_E3, 16), (S_E4, 14), (S_E5, 13), (S_UP, 2), (S_E1, 22), (S_E2, 19), (S_E3, 17), (S_E4, 15), (S_E5, 14),
+    (S_E1, 23), (S_E2, 20), (S_E3, 18), (S_E4, 16), (S_E5, 15), (S_UP, 3), (S_E2, 21), (S_E3, 19), (S_E4, 17), (S_E5, 16),
+    (S_E2, 22), (S_E3, 20), (S_E4, 18), (S_E5, 17), (S_DOWN, 0), (S_E2, 23), (S_E3, 21), (S_E4, 19), (S_E5, 18), (S_E3, 22),
+    (S_E4, 20), (S_E5, 19), (S_DOWN, 1), (S_E3, 23), (S_E4, 21), (S_E5, 20), (S_E4, 22), (S_E5, 21), (S_DOWN, 2), (S_E4, 23),
+    (S_E5, 22), (S_E5, 23), (S_DOWN, 3), (S_NORM2, 0), (S_GDOWN, 0), (S_R0, 0), (S_R0, 1), (S_GDOWN, 1), (S_R0, 2), (S_R0, 3),
+    (S_R1, 0), (S_GDOWN, 2), (S_R1, 1), (S_R0, 4), (S_R1, 2), (S_GACT, 0), (S_R1, 3), (S_GDOWN, 3), (S_R1, 4), (S_GACT, 1),
+    (S_R2A, 1), (S_GACT, 2), (S_R2A, 2), (S_GACT, 3), (S_R0, 5), (S_R2A, 0), (S_GIN, 0), (S_R2A, 3), (S_R2B, 1), (S_R2B, 2),
+    (S_GNORM, 0), (S_R1, 5), (S_GIN, 1), (S_R0, 6), (S_R2A, 4), (S_GNORM, 1), (S_R2B, 3), (S_R3B, 2), (S_R3B, 1), (S_GIN, 2),
+    (S_R1, 6), (S_R0, 7), (S_GNORM, 2), (S_R2A, 5), (S_R2B, 4), (S_GIN, 3), (S_R0, 8), (S_R1, 7), (S_R3B, 3), (S_R2B, 5),
+    (S_R3A, 4), (S_GNORM, 3), (S_R1, 8), (S_R0, 9), (S_R2B, 6), (S_R2A, 6), (S_NORM1, 0), (S_GOUT, 0), (S_R0, 10), (S_R3B, 4),
+    (S_GCTX, 0), (S_R2B, 7), (S_R1, 9), (S_R1, 10), (S_R2A, 7), (S_ABACK, 0), (S_R2B, 8), (S_R3B, 5), (S_GQKV, 0), (S_R0, 11),
+    (S_R2A, 8), (S_ABACK, 1), (S_R3B, 6), (S_R3A, 1), (S_R1, 11), (S_R3B, 7), (S_R4A, 4), (S_R3A, 6), (S_GQKV, 1), (S_R3A, 3),
+    (S_R2A, 9), (S_R0, 12), (S_ABACK, 2), (S_R2A, 10), (S_R2B, 11), (S_R1, 12), (S_GX, 0), (S_R2B, 9), (S_R3B, 8), (S_GQKV, 2),
+    (S_R3A, 2), (S_GGRADS, 0), (S_R2A, 11), (S_R0, 13), (S_R3A, 7), (S_R4B, 6), (S_R4B, 4), (S_R4B, 1), (S_R1, 13), (S_R4A, 3),
+    (S_R4A, 1), (S_R3B, 11), (S_R2B, 0), (S_R2A, 12), (S_R3A, 8), (S_R4B, 5), (S_GX, 1), (S_R4A, 2), (S_R4B, 8), (S_R3A, 9),
+    (S_R4A, 6), (S_R3B, 9), (S_R2B, 12), (S_R2B, 13), (S_GX, 2), (S_R3A, 0), (S_R2A, 13), (S_R3A, 5), (S_R2B, 10), (S_R3A, 11),
+    (S_R4B, 2), (S_R3A, 10), (S_R3B, 12), (S_R5, 5), (S_R4B, 11), (S_R4B, 7), (S_R4B, 3), (S_R3B, 13), (S_R4A, 9), (S_R3B, 10),
+    (S_R3A, 12), (S_R3B, 0), (S_R5, 8), (S_R4A, 10), (S_R4A, 5), (S_R4A, 11), (S_R4A, 8), (S_R5, 2), (S_R5, 11), (S_R4B, 12),
+    (S_R5, 3), (S_R4B, 9), (S_R4A, 7), (S_R3A, 13), (S_R4B, 13), (S_R4A, 0), (S_R5, 6), (S_R4B, 10), (S_R5, 12), (S_R4B, 0),
+    (S_R4A, 12), (S_R5, 1), (S_R5, 7), (S_R4A, 13), (S_R5, 9), (S_R5, 13), (S_R5, 4), (S_R5, 10), (S_R5, 0),
 )
 SQRT_HALF = 0.7071067811865476
 INV_SQRT_TAU = 0.3989422804014327
@@ -316,10 +318,12 @@
         loop(3, tile)
         vt[grouped, :] = qkv[g, :, 2 * group :].T
 
-    def attend(g):
+    def attend(half_group):
+        g, first = half_group // 2, half_group % 2 * 2
         length = len_ref[0]
 
-        def one(h):
+        def one(i):
+            h = first + i
             cols = span(h // 2, pair)
             keys = pl.ds(pl.multiple_of(group + (h // 2) * pair, pair), pair)
             lane = lax.broadcasted_iota(jnp.int32, (seq, pair), 1) // head
@@ -333,7 +337,7 @@
             mine = pl.ds(pl.multiple_of(g * group + h * head, head), head)
             ct[mine, :] = dot(vt[mine, :], probs).astype(BF)
 
-        loop(group // head, one)
+        loop(2, one)
 
     def out_proj(_):
         context = ct[...].T

time: 153 us -> 150 us (0.980)
  Pallas kernels: 151 us -> 148 us
    pallas_call x1, Pallas kernels: 148 us -> 145 us  [fused_layer(): pl.pallas_call(layer_kernel, out_shape=(shape(tokens.shape, BF), shape(to...]
where the time goes in v1:
time: 150 us; the launch traced here: 149 us
  Pallas kernels  148 us (99%)
    pallas_call x1, Pallas kernels, fused_layer(): pl.pallas_call(layer_kernel, out_shape=(shape(tokens.shape, BF), shape(to...  145 us
    pallas_call x1, Pallas kernels, fused_layer(): pl.pallas_call(functools.partial(place_kernel, cuts), out_shape=(*(shape(...  3.34 us

profile of v1, /device:TPU:0, one launch (start us, length us, event | category | flops | bytes accessed | tf_op | source)
XLA Modules:
  0.0 149.4 jit_solution(88205174793955370)
XLA Ops:
  1.3 144.6 %layer.1 = (bf16[1,512,768]{2,1,0:T(8,128)(2,1)}, f32[1,512,768]{2,1,0:T(8,128)}, f32[48,2304]{1,0:T(8,128)}, f32[48,768]{1,0:T(8,128)}, f32[48,3072]{1,0:T(8,12...) custom-call(bf16[1,512,768]{2,1,0:T(8,128)(2,1)} %x_hbm.1, s32[1]{0:T(128)S(6)} %copy.15.len_ref, ...), custom_call_target="tpu_custom_call" | custom-call | tf_op jit(solution)/shard_map/layer/pallas_call | solution.py:837
  145.9 3.3 %place.1 = (bf16[1,512,768]{2,1,0:T(8,128)(2,1)}, f32[1,512,768]{2,1,0:T(8,128)}, f32[48,2304]{1,0:T(8,128)}, f32[48,768]{1,0:T(8,128)}, f32[48,3072]{1,0:T(8,128)}, /*index=5*/f32[192,768]{1,0:T(8,128)}, f32[576]{0:T(1024)}) custom-call(bf16[1,512,768]{2,1,0:T(8,128)(2,1)} %get-tuple-element.14.refs_0_, f32[1,512,768]{2,1,0:T(8,128)} %get-tuple-element.15.refs_1_, ...), custom_call_target="tpu_custom_call" | custom-call | tf_op jit(solution)/shard_map/place/pallas_call | solution.py:857

commit v2 on v1

--- a/solution.py
+++ b/solution.py
@@ -26,45 +26,47 @@
 GATHERED = (
     (0, 0, 384), (0, 384, 384), (1, 0, 384), (1, 384, 384), (2, 0, 384), (2, 384, 384), (3, 0, 384), (3, 384, 384),
     (4, 0, 384), (4, 384, 384), (5, 0, 384), (5, 384, 384), (6, 0, 384), (6, 384, 384), (7, 0, 384), (7, 384, 384),
-    (8, 0, 384), (8, 384, 384), (9, 0, 384), (9, 384, 384), (10, 0, 384), (10, 384, 384), (11, 0, 384), (11, 384, 384),
+    (8, 0, 384), (8, 384, 384), (9, 0, 384), (9, 384, 384), (10, 0, 384), (10, 384, 384), (11, 0, 256), (11, 256, 256),
+    (11, 512, 256),
 )
 SUMMED = (
     (0, 0, 128), (0, 128, 128), (0, 256, 128), (1, 0, 384), (2, 0, 384), (3, 0, 384), (4, 0, 384), (5, 0, 384),
     (6, 0, 384), (7, 0, 384), (8, 0, 384), (9, 0, 384), (10, 0, 384), (11, 0, 384),
 )
 ORDER = (
-    (S_E1, 0), (S_EO, 0), (S_E1, 1), (S_EO, 1), (S_E1, 2), (S_EO, 2), (S_EO, 3), (S_EO, 4), (S_EO, 5), (S_E1, 3),
-    (S_E2, 0), (S_EO, 6), (S_E1, 4), (S_E2, 1), (S_EO, 7), (S_E1, 5), (S_E2, 2), (S_EO, 8), (S_E3, 0), (S_E1, 6),
-    (S_E2, 3), (S_EO, 9), (S_E3, 1), (S_E1, 7), (S_E2, 4), (S_EO, 10), (S_E3, 2), (S_E4, 0), (S_E1, 8), (S_E2, 5),
-    (S_EO, 11), (S_E3, 3), (S_E4, 1), (S_E5, 0), (S_E1, 9), (S_E2, 6), (S_EO, 12), (S_E3, 4), (S_E4, 2), (S_E5, 1),
-    (S_SPREAD, 0), (S_PROJECT, 0), (S_E1, 10), (S_E2, 7), (S_EO, 13), (S_E3, 5), (S_E4, 3), (S_E5, 2), (S_ATTEND, 0), (S_E1, 11),
-    (S_E2, 8), (S_EO, 14), (S_E3, 6), (S_E4, 4), (S_E5, 3), (S_ATTEND, 1), (S_E1, 12), (S_E2, 9), (S_EO, 15), (S_E3, 7),
-    (S_E4, 5), (S_E5, 4), (S_PROJECT, 1), (S_E1, 13), (S_E2, 10), (S_EO, 16), (S_E3, 8), (S_E4, 6), (S_E5, 5), (S_ATTEND, 2),
-    (S_E1, 14), (S_E2, 11), (S_EO, 17), (S_E3, 9), (S_E4, 7), (S_E5, 6), (S_ATTEND, 3), (S_E1, 15), (S_E2, 12), (S_EO, 18),
-    (S_E3, 10), (S_E4, 8), (S_E5, 7), (S_PROJECT, 2), (S_E1, 16), (S_E2, 13), (S_EO, 19), (S_E3, 11), (S_E4, 9), (S_E5, 8),
-    (S_ATTEND, 4), (S_E1, 17), (S_E2, 14), (S_EO, 20), (S_E3, 12), (S_E4, 10), (S_E5, 9), (S_ATTEND, 5), (S_E1, 18), (S_E2, 15),
-    (S_EO, 21), (S_E3, 13), (S_E4, 11), (S_E5, 10), (S_OUT, 0), (S_E1, 19), (S_E2, 16), (S_EO, 22), (S_E3, 14), (S_E4, 12),
-    (S_E5, 11), (S_UP, 0), (S_E1, 20), (S_E2, 17), (S_EO, 23), (S_E3, 15), (S_E4, 13), (S_E5, 12), (S_UP, 1), (S_E1, 21),
-    (S_E2, 18), (S_E3, 16), (S_E4, 14), (S_E5, 13), (S_UP, 2), (S_E1, 22), (S_E2, 19), (S_E3, 17), (S_E4, 15), (S_E5, 14),
-    (S_E1, 23), (S_E2, 20), (S_E3, 18), (S_E4, 16), (S_E5, 15), (S_UP, 3), (S_E2, 21), (S_E3, 19), (S_E4, 17), (S_E5, 16),
-    (S_E2, 22), (S_E3, 20), (S_E4, 18), (S_E5, 17), (S_DOWN, 0), (S_E2, 23), (S_E3, 21), (S_E4, 19), (S_E5, 18), (S_E3, 22),
-    (S_E4, 20), (S_E5, 19), (S_DOWN, 1), (S_E3, 23), (S_E4, 21), (S_E5, 20), (S_E4, 22), (S_E5, 21), (S_DOWN, 2), (S_E4, 23),
-    (S_E5, 22), (S_E5, 23), (S_DOWN, 3), (S_NORM2, 0), (S_GDOWN, 0), (S_R0, 0), (S_R0, 1), (S_GDOWN, 1), (S_R0, 2), (S_R0, 3),
-    (S_R1, 0), (S_GDOWN, 2), (S_R1, 1), (S_R0, 4), (S_R1, 2), (S_GACT, 0), (S_R1, 3), (S_GDOWN, 3), (S_R1, 4), (S_GACT, 1),
-    (S_R2A, 1), (S_GACT, 2), (S_R2A, 2), (S_GACT, 3), (S_R0, 5), (S_R2A, 0), (S_GIN, 0), (S_R2A, 3), (S_R2B, 1), (S_R2B, 2),
-    (S_GNORM, 0), (S_R1, 5), (S_GIN, 1), (S_R0, 6), (S_R2A, 4), (S_GNORM, 1), (S_R2B, 3), (S_R3B, 2), (S_R3B, 1), (S_GIN, 2),
-    (S_R1, 6), (S_R0, 7), (S_GNORM, 2), (S_R2A, 5), (S_R2B, 4), (S_GIN, 3), (S_R0, 8), (S_R1, 7), (S_R3B, 3), (S_R2B, 5),
-    (S_R3A, 4), (S_GNORM, 3), (S_R1, 8), (S_R0, 9), (S_R2B, 6), (S_R2A, 6), (S_NORM1, 0), (S_GOUT, 0), (S_R0, 10), (S_R3B, 4),
-    (S_GCTX, 0), (S_R2B, 7), (S_R1, 9), (S_R1, 10), (S_R2A, 7), (S_ABACK, 0), (S_R2B, 8), (S_R3B, 5), (S_GQKV, 0), (S_R0, 11),
-    (S_R2A, 8), (S_ABACK, 1), (S_R3B, 6), (S_R3A, 1), (S_R1, 11), (S_R3B, 7), (S_R4A, 4), (S_R3A, 6), (S_GQKV, 1), (S_R3A, 3),
-    (S_R2A, 9), (S_R0, 12), (S_ABACK, 2), (S_R2A, 10), (S_R2B, 11), (S_R1, 12), (S_GX, 0), (S_R2B, 9), (S_R3B, 8), (S_GQKV, 2),
-    (S_R3A, 2), (S_GGRADS, 0), (S_R2A, 11), (S_R0, 13), (S_R3A, 7), (S_R4B, 6), (S_R4B, 4), (S_R4B, 1), (S_R1, 13), (S_R4A, 3),
-    (S_R4A, 1), (S_R3B, 11), (S_R2B, 0), (S_R2A, 12), (S_R3A, 8), (S_R4B, 5), (S_GX, 1), (S_R4A, 2), (S_R4B, 8), (S_R3A, 9),
-    (S_R4A, 6), (S_R3B, 9), (S_R2B, 12), (S_R2B, 13), (S_GX, 2), (S_R3A, 0), (S_R2A, 13), (S_R3A, 5), (S_R2B, 10), (S_R3A, 11),
-    (S_R4B, 2), (S_R3A, 10), (S_R3B, 12), (S_R5, 5), (S_R4B, 11), (S_R4B, 7), (S_R4B, 3), (S_R3B, 13), (S_R4A, 9), (S_R3B, 10),
-    (S_R3A, 12), (S_R3B, 0), (S_R5, 8), (S_R4A, 10), (S_R4A, 5), (S_R4A, 11), (S_R4A, 8), (S_R5, 2), (S_R5, 11), (S_R4B, 12),
-    (S_R5, 3), (S_R4B, 9), (S_R4A, 7), (S_R3A, 13), (S_R4B, 13), (S_R4A, 0), (S_R5, 6), (S_R4B, 10), (S_R5, 12), (S_R4B, 0),
-    (S_R4A, 12), (S_R5, 1), (S_R5, 7), (S_R4A, 13), (S_R5, 9), (S_R5, 13), (S_R5, 4), (S_R5, 10), (S_R5, 0),
+    (S_E1, 0), (S_EO, 0), (S_E1, 1), (S_EO, 1), (S_E1, 2), (S_EO, 2), (S_EO, 3), (S_EO, 4), (S_EO, 5), (S_EO, 6),
+    (S_EO, 7), (S_E1, 3), (S_E2, 0), (S_EO, 8), (S_E1, 4), (S_E2, 1), (S_EO, 9), (S_E1, 5), (S_E2, 2), (S_EO, 10),
+    (S_E3, 0), (S_E1, 6), (S_E2, 3), (S_EO, 11), (S_E3, 1), (S_E1, 7), (S_E2, 4), (S_EO, 12), (S_E3, 2), (S_E4, 0),
+    (S_E1, 8), (S_E2, 5), (S_EO, 13), (S_E3, 3), (S_E4, 1), (S_E5, 0), (S_E1, 9), (S_E2, 6), (S_EO, 14), (S_E3, 4),
+    (S_E4, 2), (S_E5, 1), (S_SPREAD, 0), (S_PROJECT, 0), (S_E1, 10), (S_E2, 7), (S_EO, 15), (S_E3, 5), (S_E4, 3), (S_E5, 2),
+    (S_ATTEND, 0), (S_E1, 11), (S_E2, 8), (S_EO, 16), (S_E3, 6), (S_E4, 4), (S_E5, 3), (S_ATTEND, 1), (S_E1, 12), (S_E2, 9),
+    (S_EO, 17), (S_E3, 7), (S_E4, 5), (S_E5, 4), (S_PROJECT, 1), (S_E1, 13), (S_E2, 10), (S_EO, 18), (S_E3, 8), (S_E4, 6),
+    (S_E5, 5), (S_ATTEND, 2), (S_E1, 14), (S_E2, 11), (S_EO, 19), (S_E3, 9), (S_E4, 7), (S_E5, 6), (S_ATTEND, 3), (S_E1, 15),
+    (S_E2, 12), (S_EO, 20), (S_E3, 10), (S_E4, 8), (S_E5, 7), (S_PROJECT, 2), (S_E1, 16), (S_E2, 13), (S_EO, 21), (S_E3, 11),
+    (S_E4, 9), (S_E5, 8), (S_ATTEND, 4), (S_E1, 17), (S_E2, 14), (S_EO, 22), (S_E3, 12), (S_E4, 10), (S_E5, 9), (S_ATTEND, 5),
+    (S_E1, 18), (S_E2, 15), (S_EO, 23), (S_E3, 13), (S_E4, 11), (S_E5, 10), (S_OUT, 0), (S_E1, 19), (S_E2, 16), (S_EO, 24),
+    (S_E3, 14), (S_E4, 12), (S_E5, 11), (S_UP, 0), (S_E1, 20), (S_E2, 17), (S_E3, 15), (S_E4, 13), (S_E5, 12), (S_UP, 1),
+    (S_E1, 21), (S_E2, 18), (S_E3, 16), (S_E4, 14), (S_E5, 13), (S_UP, 2), (S_E1, 22), (S_E2, 19), (S_E3, 17), (S_E4, 15),
+    (S_E5, 14), (S_E1, 23), (S_E2, 20), (S_E3, 18), (S_E4, 16), (S_E5, 15), (S_UP, 3), (S_E1, 24), (S_E2, 21), (S_E3, 19),
+    (S_E4, 17), (S_E5, 16), (S_E2, 22), (S_E3, 20), (S_E4, 18), (S_E5, 17), (S_DOWN, 0), (S_E2, 23), (S_E3, 21), (S_E4, 19),
+    (S_E5, 18), (S_E2, 24), (S_E3, 22), (S_E4, 20), (S_E5, 19), (S_DOWN, 1), (S_E3, 23), (S_E4, 21), (S_E5, 20), (S_E3, 24),
+    (S_E4, 22), (S_E5, 21), (S_DOWN, 2), (S_E4, 23), (S_E5, 22), (S_E4, 24), (S_E5, 23), (S_E5, 24), (S_DOWN, 3), (S_NORM2, 0),
+    (S_GDOWN, 0), (S_R0, 0), (S_R0, 1), (S_GDOWN, 1), (S_R0, 2), (S_R0, 3), (S_R1, 0), (S_GDOWN, 2), (S_R1, 1), (S_R0, 4),
+    (S_R1, 2), (S_GACT, 0), (S_R1, 3), (S_GDOWN, 3), (S_R1, 4), (S_GACT, 1), (S_R2A, 1), (S_GACT, 2), (S_R2A, 2), (S_GACT, 3),
+    (S_R0, 5), (S_R2A, 0), (S_GIN, 0), (S_R2A, 3), (S_R2B, 1), (S_R2B, 2), (S_GNORM, 0), (S_R1, 5), (S_GIN, 1), (S_R0, 6),
+    (S_R2A, 4), (S_GNORM, 1), (S_R2B, 3), (S_R3B, 2), (S_R3B, 1), (S_GIN, 2), (S_R1, 6), (S_R0, 7), (S_GNORM, 2), (S_R2A, 5),
+    (S_R2B, 4), (S_GIN, 3), (S_R0, 8), (S_R1, 7), (S_R3B, 3), (S_R2B, 5), (S_R3A, 4), (S_GNORM, 3), (S_R1, 8), (S_R0, 9),
+    (S_R2B, 6), (S_R2A, 6), (S_NORM1, 0), (S_GOUT, 0), (S_R0, 10), (S_R3B, 4), (S_GCTX, 0), (S_R2B, 7), (S_R1, 9), (S_R1, 10),
+    (S_R2A, 7), (S_ABACK, 0), (S_R2B, 8), (S_R3B, 5), (S_GQKV, 0), (S_R0, 11), (S_R2A, 8), (S_ABACK, 1), (S_R3B, 6), (S_R3A, 1),
+    (S_R1, 11), (S_R3B, 7), (S_R4A, 4), (S_R3A, 6), (S_GQKV, 1), (S_R3A, 3), (S_R2A, 9), (S_R0, 12), (S_ABACK, 2), (S_R2A, 10),
+    (S_R2B, 11), (S_R1, 12), (S_GX, 0), (S_R2B, 9), (S_R3B, 8), (S_GQKV, 2), (S_R3A, 2), (S_GGRADS, 0), (S_R2A, 11), (S_R0, 13),
+    (S_R3A, 7), (S_R4B, 6), (S_R4B, 4), (S_R4B, 1), (S_R1, 13), (S_R4A, 3), (S_R4A, 1), (S_R3B, 11), (S_R2B, 0), (S_R2A, 12),
+    (S_R3A, 8), (S_R4B, 5), (S_GX, 1), (S_R4A, 2), (S_R4B, 8), (S_R3A, 9), (S_R4A, 6), (S_R3B, 9), (S_R2B, 12), (S_R2B, 13),
+    (S_GX, 2), (S_R3A, 0), (S_R2A, 13), (S_R3A, 5), (S_R2B, 10), (S_R3A, 11), (S_R4B, 2), (S_R3A, 10), (S_R3B, 12), (S_R5, 5),
+    (S_R4B, 11), (S_R4B, 7), (S_R4B, 3), (S_R3B, 13), (S_R4A, 9), (S_R3B, 10), (S_R3A, 12), (S_R3B, 0), (S_R5, 8), (S_R4A, 10),
+    (S_R4A, 5), (S_R4A, 11), (S_R4A, 8), (S_R5, 2), (S_R5, 11), (S_R4B, 12), (S_R5, 3), (S_R4B, 9), (S_R4A, 7), (S_R3A, 13),
+    (S_R4B, 13), (S_R4A, 0), (S_R5, 6), (S_R4B, 10), (S_R5, 12), (S_R4B, 0), (S_R4A, 12), (S_R5, 1), (S_R5, 7), (S_R4A, 13),
+    (S_R5, 9), (S_R5, 13), (S_R5, 4), (S_R5, 10), (S_R5, 0),
 )
 SQRT_HALF = 0.7071067811865476
 INV_SQRT_TAU = 0.3989422804014327

time: 150 us -> 149 us (level)
  no operation moved by 1% of the time
where the time goes in v2:
time: 149 us
  Pallas kernels  148 us (99%)
    pallas_call x1, Pallas kernels, fused_layer(): pl.pallas_call(layer_kernel, out_shape=(shape(tokens.shape, BF), shape(to...  144 us
    pallas_call x1, Pallas kernels, fused_layer(): pl.pallas_call(functools.partial(place_kernel, cuts), out_shape=(*(shape(...  3.34 us

profile of v2, /device:TPU:0, one launch (start us, length us, event | category | flops | bytes accessed | tf_op | source)
XLA Modules:
  0.0 149.0 jit_solution(13871934420726362039)
XLA Ops:
  1.3 144.2 %layer.1 = (bf16[1,512,768]{2,1,0:T(8,128)(2,1)}, f32[1,512,768]{2,1,0:T(8,128)}, f32[48,2304]{1,0:T(8,128)}, f32[48,768]{1,0:T(8,128)}, f32[48,3072]{1,0:T(8,12...) custom-call(bf16[1,512,768]{2,1,0:T(8,128)(2,1)} %x_hbm.1, s32[1]{0:T(128)S(6)} %copy.15.len_ref, ...), custom_call_target="tpu_custom_call" | custom-call | tf_op jit(solution)/shard_map/layer/pallas_call | solution.py:839
  145.5 3.3 %place.1 = (bf16[1,512,768]{2,1,0:T(8,128)(2,1)}, f32[1,512,768]{2,1,0:T(8,128)}, f32[48,2304]{1,0:T(8,128)}, f32[48,768]{1,0:T(8,128)}, f32[48,3072]{1,0:T(8,128)}, /*index=5*/f32[192,768]{1,0:T(8,128)}, f32[576]{0:T(1024)}) custom-call(bf16[1,512,768]{2,1,0:T(8,128)(2,1)} %get-tuple-element.14.refs_0_, f32[1,512,768]{2,1,0:T(8,128)} %get-tuple-element.15.refs_1_, ...), custom_call_target="tpu_custom_call" | custom-call | tf_op jit(solution)/shard_map/place/pallas_call | solution.py:859
